TPU v7x, 32 devices: a whole 2x2x4 slice. The times are simulated.
32 devices in a mesh: row: 8 (over y, x, core), rep: 4 (over z).
Axes of the slice: x: 2, y: 2, z: 4, core: 2. Of those that a mesh axis runs over, the one named last changes fastest.
Arguments:
- node_feats: bfloat16 [8192, 1024], P('row'), may hold values from -6 to 6
- block_cols: int32 [64, 4], P('row'), may hold values from -1 to 63, as said below
- block_vals: bfloat16 [64, 4, 128, 128], P('row'), may hold values from -0.26367188 to 0.26367188
- w_in: bfloat16 [1024, 4096], P(None, 'rep'), may hold values from -0.1875 to 0.1875
- w_out: bfloat16 [1024, 4096], P(None, 'rep'), may hold values from -0.09375 to 0.09375
- cotangent: bfloat16 [8192, 1024], P('row', 'rep'), may hold values from -6 to 6
Outputs:
- updated: bfloat16 [8192, 1024], P('row', 'rep')
- grad_nodes: bfloat16 [8192, 1024], P('row', 'rep')
Inputs may be any that keep to these rules, and one draw needn't show every extreme that they name: `block_cols`: slot 0 of block-row b holds b itself. Every other present block-column lies within 16 block-rows of its block-row; absent slots hold -1, and the number of present blocks differs from block-row to block-row. A pair of block-row and block-column may repeat.
All inputs are finite; a program needn't handle non-finite values.
Results may differ from a plain program's by a relative error of at most 0.013.
Values may be sent and summed in bfloat16 or wider, within the bound.
A program may use at most 128 MiB of HBM per device.

v0:
```python
import jax
import jax.numpy as jnp
from jax import lax
from jax.sharding import PartitionSpec as P


def passed_along(value, axis, steps):
    count = lax.axis_size(axis)
    first, last = (max(0, -steps), min(count, count - steps))
    return lax.ppermute(value, axis, [(source, source + steps) for source in range(first, last)])


def gelu_value(values):
    cubic_arg = 0.7978845608 * (values + 0.044715 * values * values * values)
    return 0.5 * values * (1.0 + jnp.tanh(cubic_arg))


def gelu_slope(values):
    cubic_arg = 0.7978845608 * (values + 0.044715 * values * values * values)
    tangent = jnp.tanh(cubic_arg)
    return 0.5 * (1.0 + tangent) + 0.5 * values * (1.0 - tangent * tangent) * 0.7978845608 * (
        1.0 + 3.0 * 0.044715 * values * values
    )


def aggregate(extended, block_vals, present, position):
    feat_width = extended.shape[1]
    panels = extended.reshape(-1, 128, feat_width)
    picked = panels[position]
    picked = jnp.where(present[:, :, None, None], picked, jnp.zeros((), picked.dtype))
    summed = jnp.einsum("rsij,rsjf->rif", block_vals, picked, preferred_element_type=jnp.float32)
    return summed.reshape(-1, feat_width)


def body(node_feats, block_cols, block_vals, w_in, w_out, cotangent):
    local_rows = node_feats.shape[0]
    row_blocks = local_rows // 128
    quarter = cotangent.shape[1]
    first_block = (lax.axis_index("row") - 2) * row_blocks
    rep_index = lax.axis_index("rep")
    own_quarter = lax.dynamic_slice_in_dim(node_feats, rep_index * quarter, quarter, 1)
    present = block_cols >= 0
    position = jnp.where(present, block_cols - first_block, 0)
    received = []
    for offset in (2, 1, -1, -2):
        received.append(passed_along(node_feats, "row", offset))
    extended = jnp.concatenate(received[:2] + [node_feats] + received[2:], axis=0)
    gathered = aggregate(extended, block_vals, present, position).astype(jnp.bfloat16)
    pre_act = jnp.dot(gathered, w_in, preferred_element_type=jnp.float32)
    hidden = gelu_value(pre_act).astype(jnp.bfloat16)
    partial_out = lax.dot_general(
        hidden, w_out, (((1,), (1,)), ((), ())), preferred_element_type=jnp.float32
    )
    summed_out = lax.psum_scatter(
        partial_out.astype(jnp.bfloat16), "rep", scatter_dimension=1, tiled=True
    ).astype(jnp.float32)
    updated = (own_quarter.astype(jnp.float32) + summed_out).astype(jnp.bfloat16)
    grad_hidden = jnp.dot(
        lax.all_gather(cotangent, "rep", axis=1, tiled=True),
        w_out,
        preferred_element_type=jnp.float32,
    )
    grad_pre = (grad_hidden * gelu_slope(pre_act)).astype(jnp.bfloat16)
    partial_adj = lax.dot_general(
        grad_pre, w_in, (((1,), (1,)), ((), ())), preferred_element_type=jnp.float32
    )
    adjoint = lax.psum_scatter(
        partial_adj.astype(jnp.bfloat16), "rep", scatter_dimension=1, tiled=True
    )
    adjoint_blocks = adjoint.reshape(row_blocks, 128, quarter)
    contrib = jnp.einsum(
        "rsji,rjf->rsif", block_vals, adjoint_blocks, preferred_element_type=jnp.float32
    )
    slot_count = block_cols.shape[1]
    flat_contrib = contrib.reshape(row_blocks * slot_count, 128 * quarter)
    landing_ids = jnp.arange(5 * row_blocks, dtype=jnp.int32)[:, None]
    one_hot = ((landing_ids == position.reshape(1, -1)) & present.reshape(1, -1)).astype(
        jnp.float32
    )
    landing = jnp.dot(
        one_hot, flat_contrib, precision=lax.Precision.HIGHEST, preferred_element_type=jnp.float32
    )
    pieces = landing.reshape(5, local_rows, quarter)
    running = pieces[2]
    for offset in (-2, -1, 1, 2):
        running = running + passed_along(
            pieces[offset + 2].astype(jnp.bfloat16), "row", offset
        ).astype(jnp.float32)
    grad_nodes = (cotangent.astype(jnp.float32) + running).astype(jnp.bfloat16)
    return (updated, grad_nodes)


def solution(mesh):
    in_specs = (
        P("row", None),
        P("row", None),
        P("row", None, None, None),
        P(None, "rep"),
        P(None, "rep"),
        P("row", "rep"),
    )
    out_specs = (P("row", "rep"), P("row", "rep"))
    return jax.shard_map(body, mesh=mesh, in_specs=in_specs, out_specs=out_specs, check_vma=False)
```

profile of v0, /device:TPU:28, one launch (start us, length us, event | category | flops | bytes accessed | tf_op | source)
XLA Modules:
  0.0 285.1 jit_solution(17277032886436098723)
XLA Ops:
  7.2 0.0 all-gather.2.cloned.1.call-start
  7.2 3.5 %collective-permute-start = (bf16[1024,1024]{1,0:T(8,128)(2,1)}, bf16[1024,1024]{1,0:T(8,128)(2,1)}, u32[]{:S(2)}, u32[]{:S(2)}) collective-permute-start(bf16[1024,1024]{1,0:T(8,128)(2,1)} %param.6), channel_id=1, source_target_pairs={{0,8},{4,12},{8,16},{12,20},{16,24},{20,28},{1,9},{5,13},{9,17},{1... | collective-permute-start | bytes 6291464 | tf_op jit(solution)/shard_map/ppermute | solution.py:10
  10.8 1.9 collective-permute-start.1
  12.7 4.5 %collective-permute-start.2 = (bf16[1024,1024]{1,0:T(8,128)(2,1)}, bf16[1024,1024]{1,0:T(8,128)(2,1)}, u32[]{:S(2)}, u32[]{:S(2)}) collective-permute-start(bf16[1024,1024]{1,0:T(8,128)(2,1)} %param.6), channel_id=1, source_target_pairs={{4,0},{8,4},{12,8},{16,12},{20,16},{24,20},{28,24},{5,1},{9,5},{13... | collective-permute-start | bytes 6291464 | tf_op jit(solution)/shard_map/ppermute | solution.py:10
  17.3 2.4 collective-permute-start.3
  19.7 0.0 all-gather.2.cloned.1.call-update
  19.7 0.0 reduce-scatter.5.cloned.1.call-start
  19.8 0.7 compare_select_fusion
  20.5 0.1 copy.14
  20.6 0.1 reshape.40
  20.6 0.7 broadcast_compare_fusion
  21.3 0.1 copy.13
  21.4 37.5 %collective-permute-done = bf16[1024,1024]{1,0:T(8,128)(2,1)} collective-permute-done((bf16[1024,1024]{1,0:T(8,128)(2,1)}, bf16[1024,1024]{1,0:T(8,128)(2,1)}, u32[]{:S(2)}, u32[]{:S(2)}) %collective-permute-start) | collective-permute-done | bytes 2097184 | tf_op jit(solution)/shard_map/ppermute | solution.py:10
  59.0 3.1 %constant_dynamic-update-slice_fusion.4 = bf16[5120,1024]{1,0:T(8,128)(2,1)} fusion(bf16[1024,1024]{1,0:T(8,128)(2,1)} %collective-permute-done), kind=kLoop, calls=%fused_computation.33 | loop fusion | bytes 4194304
  62.1 39.5 %collective-permute-done.1 = bf16[1024,1024]{1,0:T(8,128)(2,1)} collective-permute-done((bf16[1024,1024]{1,0:T(8,128)(2,1)}, bf16[1024,1024]{1,0:T(8,128)(2,1)}, u32[]{:S(2)}, u32[]{:S(2)}) %collective-permute-start.1) | collective-permute-done | bytes 2097184 | tf_op jit(solution)/shard_map/ppermute | solution.py:10
  101.6 3.1 %constant_dynamic-update-slice_fusion.3 = bf16[5120,1024]{1,0:T(8,128)(2,1)} fusion(bf16[5120,1024]{1,0:T(8,128)(2,1)} %constant_dynamic-update-slice_fusion.4, bf16[1024,1024]{1,0:T(8,128)(2,1)} %collective-permute-done.1), kind=kLoop, calls=%fused_computation.32 | loop fusion | bytes 4194304
  104.7 1.5 constant_dynamic-update-slice_fusion.2
  106.2 3.1 %constant_dynamic-update-slice_fusion.1 = bf16[5120,1024]{1,0:T(8,128)(2,1)} fusion(bf16[5120,1024]{1,0:T(8,128)(2,1)} %constant_dynamic-update-slice_fusion.2, bf16[1024,1024]{1,0:T(8,128)(2,1)} %collective-permute-done.2), kind=kLoop, calls=%fused_computation.30 | loop fusion | bytes 4194304
  109.4 36.5 %collective-permute-done.3 = bf16[1024,1024]{1,0:T(8,128)(2,1)} collective-permute-done((bf16[1024,1024]{1,0:T(8,128)(2,1)}, bf16[1024,1024]{1,0:T(8,128)(2,1)}, u32[]{:S(2)}, u32[]{:S(2)}) %collective-permute-start.3) | collective-permute-done | bytes 2097184 | tf_op jit(solution)/shard_map/ppermute | solution.py:10
  145.8 3.2 %constant_dynamic-update-slice_fusion = bf16[5120,1024]{1,0:T(8,128)(2,1)} fusion(bf16[5120,1024]{1,0:T(8,128)(2,1)} %constant_dynamic-update-slice_fusion.1, bf16[1024,1024]{1,0:T(8,128)(2,1)} %collective-permute-done.3), kind=kLoop, calls=%fused_computation.29 | loop fusion | bytes 4194304 | tf_op jit(solution)/shard_map/concatenate | solution.py:47
  149.0 9.1 %gather_fusion = bf16[32,128,1024]{2,1,0:T(8,128)(2,1)} fusion(bf16[40,128,1024]{2,1,0:T(8,128)(2,1)} %bitcast, s32[1024]{0:T(1024)S(1)} %pad_clamp_fusion), kind=kCustom, calls=%fused_computation | custom fusion | bytes 16777344 | tf_op jit(solution)/shard_map/gather | solution.py:29
  158.1 4.7 %bitcast_convert_fusion = bf16[8,1024,128]{1,2,0:T(8,128)(2,1)S(1)} fusion(bf16[8,4,128,128]{3,2,1,0:T(8,128)(2,1)S(1)} %copy-done.3, bf16[8,4,128,1024]{3,2,1,0:T(8,128)(2,1)} %bitcast.31, pred[8,4]{1,0:T(8,128)(4,1)S(1)} %copy.13), kind=kOutput, calls=%fused_computation.13 | convolution fusion | flops 1078984704 | bytes 11534368 | tf_op jit(solution)/shard_map/rsij,rsjf->rif/dot_general | solution.py:31
  162.8 4.3 %fusion.36 = f32[1024,1024]{1,0:T(8,128)} fusion(bf16[1024,1024]{1,0:T(8,128)(2,1)S(1)} %bitcast.33, bf16[1024,1024]{1,0:T(8,128)(2,1)S(1)} %copy-done), kind=kOutput, calls=%fused_computation.52 | convolution fusion | flops 2147483648 | bytes 8388608 | tf_op jit(solution)/shard_map/dot_general | solution.py:49
  167.1 8.9 %convolution_convert_fusion = bf16[1024,1024]{1,0:T(8,128)(2,1)} fusion(bf16[1024,1024]{1,0:T(8,128)(2,1)S(1)} %copy-done, f32[1024,1024]{1,0:T(8,128)} %fusion.36, bf16[1024,1024]{1,0:T(8,128)(2,1)} %all-gather.2.cloned.1.call-done, bf16[1024,1024]{1,0:T(8,128)(2,1)} %param.10), kind=kOutput, calls=%fused_computation.23 | convolution fusion | flops 4315938816 | bytes 12582912 | tf_op jit(solution)/shard_map/dot_general | solution.py:64
  176.1 0.2 reduce-scatter.3.cloned.1.call-start
  176.3 0.1 and.12
  176.4 0.1 copy.15
  176.5 0.1 eq.16
  176.6 6.8 %fusion.16 = bf16[1024,1024]{1,0:T(8,128)(2,1)} fusion(bf16[1024,1024]{1,0:T(8,128)(2,1)} %param.10, f32[1024,1024]{1,0:T(8,128)} %fusion.36), kind=kOutput, calls=%fused_computation.22 | convolution fusion | flops 2157969408 | bytes 8388608 | tf_op jit(solution)/shard_map/dot_general | solution.py:51
  183.4 37.0 %reduce-scatter.5.cloned.1.call-done = bf16[1024,256]{1,0:T(8,128)(2,1)} async-done(((bf16[1024,1024]{1,0:T(8,128)(2,1)}), bf16[1024,256]{1,0:T(8,128)(2,1)}) %reduce-scatter.5.cloned.1.call-update) | async-done | bytes 524304 | tf_op jit(solution)/shard_map/reduce_scatter | solution.py:67
  220.4 3.7 %convolution_bitcast_fusion = f32[8,4,128,256]{2,3,1,0:T(8,128)} fusion(bf16[8,128,256,1]{2,1,3,0:T(8,128)(2,1)} %bitcast.32, bf16[8,4,128,128]{3,2,1,0:T(8,128)(2,1)S(1)} %copy-done.3), kind=kOutput, calls=%fused_computation.16 | convolution fusion | flops 268435456 | bytes 5767168 | tf_op jit(solution)/shard_map/rsji,rjf->rsif/dot_general | solution.py:71
  224.1 5.5 %copy.23 = f32[4,8,128,256]{3,1,2,0:T(8,128)} copy(f32[4,8,128,256]{2,3,1,0:T(8,128)} %bitcast.30) | data formatting | bytes 8388608
  229.6 7.1 %fusion.35 = (bf16[40,32768]{1,0:T(8,128)(2,1)S(1)}, f32[40,32768]{1,0:T(8,128)}) fusion(f32[32,32768]{1,0:T(8,128)} %bitcast.29, s32[32]{0:T(128)S(1)} %eq.16, pred[32]{0:T(512)(128)(4,1)S(1)} %and.12), kind=kOutput, calls=%fused_computation.51 | convolution fusion | flops 504629760 | bytes 12058784 | tf_op jit(solution)/shard_map/dot_general | solution.py:80
  236.8 0.1 fusion.34
  236.9 1.0 convert_element_type.82
  237.9 3.4 %collective-permute-start.7 = (bf16[1024,256]{1,0:T(8,128)(2,1)}, bf16[1024,256]{1,0:T(8,128)(2,1)}, u32[]{:S(2)}, u32[]{:S(2)}) collective-permute-start(bf16[1024,256]{1,0:T(8,128)(2,1)} %convert_element_type.82), channel_id=1, source_target_pairs={{0,8},{4,12},{8,16},{12,20},{16,24},{20,28},{1,9},{5,13},{9,17},{1... | collective-permute-start | bytes 1572872 | tf_op jit(solution)/shard_map/ppermute | solution.py:10
  241.3 1.0 convert_element_type.80
  242.4 1.9 collective-permute-start.6
  244.3 1.1 convert_element_type.78
  245.4 4.5 %collective-permute-start.5 = (bf16[1024,256]{1,0:T(8,128)(2,1)}, bf16[1024,256]{1,0:T(8,128)(2,1)}, u32[]{:S(2)}, u32[]{:S(2)}) collective-permute-start(bf16[1024,256]{1,0:T(8,128)(2,1)} %convert_element_type.78), channel_id=1, source_target_pairs={{4,0},{8,4},{12,8},{16,12},{20,16},{24,20},{28,24},{5,1},{9,5},{13... | collective-permute-start | bytes 1572872 | tf_op jit(solution)/shard_map/ppermute | solution.py:10
  249.9 1.1 convert_element_type.76
  251.0 2.4 collective-permute-start.4
  253.5 12.5 %reduce-scatter.3.cloned.1.call-done = bf16[1024,256]{1,0:T(8,128)(2,1)} async-done(((bf16[1024,1024]{1,0:T(8,128)(2,1)}), bf16[1024,256]{1,0:T(8,128)(2,1)}) %reduce-scatter.3.cloned.1.call-update) | async-done | bytes 524304 | tf_op jit(solution)/shard_map/reduce_scatter | solution.py:54
  266.0 2.1 add_convert_fusion.1
  268.1 1.4 slice.31
  269.6 1.1 squeeze.2
  270.7 4.7 %collective-permute-done.4 = bf16[1024,256]{1,0:T(8,128)(2,1)} collective-permute-done((bf16[1024,256]{1,0:T(8,128)(2,1)}, bf16[1024,256]{1,0:T(8,128)(2,1)}, u32[]{:S(2)}, u32[]{:S(2)}) %collective-permute-start.4) | collective-permute-done | bytes 524320 | tf_op jit(solution)/shard_map/ppermute | solution.py:10
  275.5 3.1 %add_convert_fusion = bf16[1024,256]{1,0:T(8,128)(2,1)} fusion(bf16[1024,256]{1,0:T(8,128)(2,1)} %collective-permute-done.7, bf16[1024,256]{1,0:T(8,128)(2,1)} %collective-permute-done.6, bf16[1024,256]{1,0:T(8,128)(2,1)} %collective-permute-done.5, f32[1024,256]{1,0:T(8,128)} %squeeze.2, bf16[1024,256]{1,0:T(8,128)(2,1)} %collective-permute-done.4, ...), kind=kLoop, calls=%fused_computation.24 | loop fusion | flops 2883584 | bytes 4194304 | tf_op jit(solution)/shard_map/convert_element_type | solution.py:89
  (16 shorter events, 0.1 us)
Async XLA Ops:
  7.2 155.7 %copy-start = (bf16[1024,1024]{1,0:T(8,128)(2,1)S(1)}, bf16[1024,1024]{1,0:T(8,128)(2,1)}, u32[]{:S(2)}) copy-start(bf16[1024,1024]{1,0:T(8,128)(2,1)} %param.9) | copy-start | bytes 6291460
  7.2 160.0 %all-gather.2.cloned.1.call-start = ((), (), s32[]{:S(2)}) async-start(), calls=%async_computation.3 | async-start | bytes 2621440 | tf_op jit(solution)/shard_map/all_gather | solution.py:59
  7.2 51.8 %collective-permute-start = (bf16[1024,1024]{1,0:T(8,128)(2,1)}, bf16[1024,1024]{1,0:T(8,128)(2,1)}, u32[]{:S(2)}, u32[]{:S(2)}) collective-permute-start(bf16[1024,1024]{1,0:T(8,128)(2,1)} %param.6), channel_id=1, source_target_pairs={{0,8},{4,12},{8,16},{12,20},{16,24},{20,28},{1,9},{5,13},{9,17},{1... | collective-permute-start | bytes 6291464 | tf_op jit(solution)/shard_map/ppermute | solution.py:10
  10.8 90.9 %collective-permute-start.1 = (bf16[1024,1024]{1,0:T(8,128)(2,1)}, bf16[1024,1024]{1,0:T(8,128)(2,1)}, u32[]{:S(2)}, u32[]{:S(2)}) collective-permute-start(bf16[1024,1024]{1,0:T(8,128)(2,1)} %param.6), channel_id=1, source_target_pairs={{0,4},{4,8},{8,12},{12,16},{16,20},{20,24},{24,28},{1,5},{5,9},{9,... | collective-permute-start | bytes 6291464 | tf_op jit(solution)/shard_map/ppermute | solution.py:10
  12.7 93.6 %collective-permute-start.2 = (bf16[1024,1024]{1,0:T(8,128)(2,1)}, bf16[1024,1024]{1,0:T(8,128)(2,1)}, u32[]{:S(2)}, u32[]{:S(2)}) collective-permute-start(bf16[1024,1024]{1,0:T(8,128)(2,1)} %param.6), channel_id=1, source_target_pairs={{4,0},{8,4},{12,8},{16,12},{20,16},{24,20},{28,24},{5,1},{9,5},{13... | collective-permute-start | bytes 6291464 | tf_op jit(solution)/shard_map/ppermute | solution.py:10
  17.3 128.6 %collective-permute-start.3 = (bf16[1024,1024]{1,0:T(8,128)(2,1)}, bf16[1024,1024]{1,0:T(8,128)(2,1)}, u32[]{:S(2)}, u32[]{:S(2)}) collective-permute-start(bf16[1024,1024]{1,0:T(8,128)(2,1)} %param.6), channel_id=1, source_target_pairs={{8,0},{12,4},{16,8},{20,12},{24,16},{28,20},{9,1},{13,5},{17,9},{2... | collective-permute-start | bytes 6291464 | tf_op jit(solution)/shard_map/ppermute | solution.py:10
  19.7 200.7 %reduce-scatter.5.cloned.1.call-start = ((), (), s32[]{:S(2)}) async-start(), calls=%async_computation.4 | async-start | bytes 2621440 | tf_op jit(solution)/shard_map/reduce_scatter | solution.py:67
  21.4 83.3 %copy-start.2 = (bf16[1024,1024]{1,0:T(8,128)(2,1)S(1)}, bf16[1024,1024]{1,0:T(8,128)(2,1)}, u32[]{:S(2)}) copy-start(bf16[1024,1024]{1,0:T(8,128)(2,1)} %param.6) | copy-start | bytes 6291460
  149.0 9.1 %copy-start.3 = (bf16[8,4,128,128]{3,2,1,0:T(8,128)(2,1)S(1)}, bf16[8,4,128,128]{3,2,1,0:T(8,128)(2,1)}, u32[]{:S(2)}) copy-start(bf16[8,4,128,128]{3,2,1,0:T(8,128)(2,1)} %param.8) | copy-start | bytes 3145732
  176.1 89.9 %reduce-scatter.3.cloned.1.call-start = ((), (), s32[]{:S(2)}) async-start(), calls=%async_computation.2 | async-start | bytes 2621440 | tf_op jit(solution)/shard_map/reduce_scatter | solution.py:54
  237.9 32.8 %collective-permute-start.7 = (bf16[1024,256]{1,0:T(8,128)(2,1)}, bf16[1024,256]{1,0:T(8,128)(2,1)}, u32[]{:S(2)}, u32[]{:S(2)}) collective-permute-start(bf16[1024,256]{1,0:T(8,128)(2,1)} %convert_element_type.82), channel_id=1, source_target_pairs={{0,8},{4,12},{8,16},{12,20},{16,24},{20,28},{1,9},{5,13},{9,17},{1... | collective-permute-start | bytes 1572872 | tf_op jit(solution)/shard_map/ppermute | solution.py:10
  242.4 28.3 %collective-permute-start.6 = (bf16[1024,256]{1,0:T(8,128)(2,1)}, bf16[1024,256]{1,0:T(8,128)(2,1)}, u32[]{:S(2)}, u32[]{:S(2)}) collective-permute-start(bf16[1024,256]{1,0:T(8,128)(2,1)} %convert_element_type.80), channel_id=1, source_target_pairs={{0,4},{4,8},{8,12},{12,16},{16,20},{20,24},{24,28},{1,5},{5,9},{9,... | collective-permute-start | bytes 1572872 | tf_op jit(solution)/shard_map/ppermute | solution.py:10
  245.4 25.3 %collective-permute-start.5 = (bf16[1024,256]{1,0:T(8,128)(2,1)}, bf16[1024,256]{1,0:T(8,128)(2,1)}, u32[]{:S(2)}, u32[]{:S(2)}) collective-permute-start(bf16[1024,256]{1,0:T(8,128)(2,1)} %convert_element_type.78), channel_id=1, source_target_pairs={{4,0},{8,4},{12,8},{16,12},{20,16},{24,20},{28,24},{5,1},{9,5},{13... | collective-permute-start | bytes 1572872 | tf_op jit(solution)/shard_map/ppermute | solution.py:10
  251.0 24.5 %collective-permute-start.4 = (bf16[1024,256]{1,0:T(8,128)(2,1)}, bf16[1024,256]{1,0:T(8,128)(2,1)}, u32[]{:S(2)}, u32[]{:S(2)}) collective-permute-start(bf16[1024,256]{1,0:T(8,128)(2,1)} %convert_element_type.76), channel_id=1, source_target_pairs={{8,0},{12,4},{16,8},{20,12},{24,16},{28,20},{9,1},{13,5},{17,9},{2... | collective-permute-start | bytes 1572872 | tf_op jit(solution)/shard_map/ppermute | solution.py:10
  268.1 10.5 %copy-start.1 = (bf16[1024,1024]{1,0:T(8,128)(2,1)S(1)}, bf16[1024,1024]{1,0:T(8,128)(2,1)}, u32[]{:S(2)}) copy-start(bf16[1024,1024]{1,0:T(8,128)(2,1)} %param.9) | copy-start | bytes 6291460
Sparse Core Ops, SparseCore 0:
  19.9 45.6 all-gather.1
  176.2 44.1 reduce-scatter.4
  222.8 43.1 reduce-scatter.2
where the time goes:
time: 291 us; the launch traced here: 285 us
  waiting for transfers between devices  168 us (58%)
  local copies, waits for them, and re-layouts  36.1 us (12%)
  matrix products  35.6 us (12%)
  starting transfers between devices  25 us (9%)
  between operations  13.9 us (5%)
  other arithmetic  6.64 us (2%)
    ppermute x8, waiting for transfers between devices, passed_along(): lax.ppermute(value, axis, [(source, source + steps) for source in range(f...  118 us
    reduce_scatter x1, waiting for transfers between devices, body(): lax.psum_scatter(partial_adj.astype(jnp.bfloat16), 'rep', scatter_dimensi...  37 us
    ppermute x8, starting transfers between devices, passed_along(): lax.ppermute(value, axis, [(source, source + steps) for source in range(f...  24.7 us
    unnamed x13, local copies, waits for them, and re-layouts  16.4 us
    reduce_scatter x1, waiting for transfers between devices, body(): lax.psum_scatter(partial_out.astype(jnp.bfloat16), 'rep', scatter_dimensi...  12.5 us
    gather x1, local copies, waits for them, and re-layouts, aggregate(): picked = panels[position]  9.12 us
    dot_general x1, matrix products, body(): lax.dot_general(grad_pre, w_in, (((1,), (1,)), ((), ())), preferred_eleme...  8.9 us
    dot_general x1, matrix products, body(): jnp.dot(one_hot, flat_contrib, precision=lax.Precision.HIGHEST, preferred...  7.12 us
  transfers between devices with their start and end apart: 11, of which 6 were waited for; matrix products, arithmetic and copies ran while one was open for 23% of the time, Pallas kernels for 0%

commit v1 on v0

v1 whole, which is shorter than its diff:
```python
import functools

import jax
import jax.numpy as jnp
from jax import lax
from jax.experimental import pallas as pl
from jax.experimental.pallas import tpu as pltpu
from jax.sharding import PartitionSpec as P

F32 = jnp.float32
BF16 = jnp.bfloat16
MESH = pl.DeviceIdType.MESH


def dot(a, b, dims=((1,), (0,))):
    return lax.dot_general(a, b, (dims, ((), ())), preferred_element_type=F32)


def gelu_pair(v):
    c = 0.7978845608
    vv = v * v
    t = jnp.tanh(c * (v + 0.044715 * v * vv))
    half = 0.5 * (1.0 + t)
    value = v * half
    slope = half + 0.5 * v * (1.0 - t * t) * c * (1.0 + 3.0 * 0.044715 * vv)
    return value, slope


def kernel(
    n_row, n_rep, mask_ref, feats_ref, vals_ref, w_in_ref, w_out_ref, cot_ref,
    upd_ref, grad_ref,
    ext, vals_t, dense, dense_t, agg_acc, w2_in, w2_out, cot_full, agg, agg_full, hid, gp,
    adj_p, out_p, adj_in, out_in, adj, c_send, c_sib, c_nbr,
    loc_sem, f_send, f_recv, w_send, w_recv, a_send, a_recv, c_sends, c_recvs,
):
    r, z = lax.axis_index("row"), lax.axis_index("rep")
    k = lax.rem(r, 2)
    sib = r + 1 - 2 * k
    mate = z + 1 - 2 * lax.rem(z, 2)
    rows, quarter = cot_ref.shape
    half = rows // 2
    row_blocks = rows // 128
    slots = vals_ref.shape[1]
    feat = w_in_ref.shape[0]
    hidw = w_in_ref.shape[1]
    has_up, has_dn = r + 2 < n_row, r >= 2
    peers = [lax.rem(z + i, n_rep) for i in range(1, n_rep)]
    froms = [lax.rem(z + n_rep - i, n_rep) for i in range(1, n_rep)]

    def remote(src, dst, send, recv, dev):
        return pltpu.make_async_remote_copy(
            src_ref=src, dst_ref=dst, send_sem=send, recv_sem=recv, device_id=dev, device_id_type=MESH
        )

    def panel(ref, slot):
        return ref.at[pl.ds(pl.multiple_of(slot * rows, rows), rows)]

    def halves(ref, s):
        return ref.at[pl.ds(pl.multiple_of(s * half, half), half)]

    barrier = pltpu.get_barrier_semaphore()
    for zp in peers:
        pl.semaphore_signal(barrier, inc=1, device_id=(r, zp), device_id_type=MESH)
    pl.semaphore_signal(barrier, inc=1, device_id=(sib, z), device_id_type=MESH)

    @pl.when(has_up)
    def _():
        pl.semaphore_signal(barrier, inc=1, device_id=(r + 2, z), device_id_type=MESH)

    @pl.when(has_dn)
    def _():
        pl.semaphore_signal(barrier, inc=1, device_id=(r - 2, z), device_id_type=MESH)

    columns = pl.ds(pl.multiple_of(z * quarter, quarter), quarter)
    own_copy = pltpu.make_async_copy(feats_ref.at[:, columns], panel(ext, 2), loc_sem)
    own_copy.start()
    own_copy.wait()
    pl.semaphore_wait(barrier, n_rep + has_up.astype(jnp.int32) + has_dn.astype(jnp.int32))

    own = panel(ext, 2)
    f_up = remote(own, panel(ext, 0), f_send.at[0], f_recv.at[0], (r + 2, z))
    f_dn = remote(own, panel(ext, 4), f_send.at[1], f_recv.at[1], (r - 2, z))
    f_sib = remote(own, panel(ext, 1 + 2 * k), f_send.at[2], f_recv.at[2], (sib, z))
    f_fwd = remote(
        panel(ext, 4 - 4 * k), panel(ext, 3 - 2 * k), f_send.at[3], f_recv.at[3], (sib, z)
    )
    from_dn = remote(own, panel(ext, 0), f_send.at[0], f_recv.at[0], (r - 2, z))
    from_up = remote(own, panel(ext, 4), f_send.at[1], f_recv.at[1], (r + 2, z))
    from_sib = remote(own, panel(ext, 3 - 2 * k), f_send.at[2], f_recv.at[2], (sib, z))
    from_fwd = remote(own, panel(ext, 1 + 2 * k), f_send.at[3], f_recv.at[3], (sib, z))
    fwd_out = jnp.where(k == 0, r + 2 < n_row, r >= 2)
    fwd_in = jnp.where(k == 0, r >= 2, r + 2 < n_row)

    @pl.when(has_up)
    def _():
        f_up.start()

    @pl.when(has_dn)
    def _():
        f_dn.start()

    f_sib.start()
    cot_out = [
        remote(halves(cot_ref, lax.rem(zp, 2)), cot_full.at[z], a_send.at[0, i], a_recv.at[0, i], (r, zp))
        for i, zp in enumerate(peers)
    ]
    for copy in cot_out:
        copy.start()
    w_out1 = [
        remote(halves(src, k), halves(dst, k), w_send.at[i], w_recv.at[i], (r, mate))
        for i, (src, dst) in enumerate(((w_in_ref, w2_in), (w_out_ref, w2_out)))
    ]
    w_fwd = [
        remote(halves(dst, k), halves(dst, k), w_send.at[2 + i], w_recv.at[2 + i], (sib, z))
        for i, dst in enumerate((w2_in, w2_out))
    ]
    w_got = [
        remote(halves(dst, 1 - k), halves(dst, 1 - k), w_send.at[2 + i], w_recv.at[2 + i], (sib, z))
        for i, dst in enumerate((w2_in, w2_out))
    ]
    for copy in w_out1:
        copy.start()

    @pl.when(jnp.logical_not(has_dn))
    def _():
        ext[0:rows] = jnp.zeros((rows, quarter), BF16)

    @pl.when(jnp.logical_not(has_up))
    def _():
        ext[4 * rows : 5 * rows] = jnp.zeros((rows, quarter), BF16)

    @pl.when(r < 1)
    def _():
        ext[rows : 2 * rows] = jnp.zeros((rows, quarter), BF16)

    @pl.when(r + 1 >= n_row)
    def _():
        ext[3 * rows : 4 * rows] = jnp.zeros((rows, quarter), BF16)

    cot_full[z] = cot_ref[pl.ds(pl.multiple_of(lax.rem(z, 2) * half, half), half), :]

    def transpose_block(b, carry):
        for s in range(slots):
            vals_t[b, s] = vals_ref[b, s].astype(F32).T.astype(BF16)
        return carry

    lax.fori_loop(0, row_blocks, transpose_block, 0)

    def fill_dense(t, carry):
        at = pl.ds(pl.multiple_of(t * 128, 128), 128)
        for b in range(row_blocks):
            straight = jnp.zeros((8, 16, 128), BF16)
            turned = jnp.zeros((8, 16, 128), BF16)
            for s in range(slots):
                row = mask_ref[t, b * slots + s : b * slots + s + 1, :]
                keep = jnp.broadcast_to(row, (16, 128)).astype(BF16)[None]
                straight = straight + vals_ref[b, s].reshape(8, 16, 128) * keep
                turned = turned + vals_t[b, s].reshape(8, 16, 128) * keep
            dense[b * 128 : (b + 1) * 128, at] = straight.reshape(128, 128)
            dense_t[at, b * 128 : (b + 1) * 128] = turned.reshape(128, 128)
        return carry

    lax.fori_loop(0, 5 * row_blocks, fill_dense, 0)

    def gather(slot, first=False):
        inner = pl.ds(pl.multiple_of(slot * rows, rows), rows)

        def step(m, carry):
            at = pl.ds(pl.multiple_of(m * 256, 256), 256)
            part = dot(dense[at, inner], ext[inner, :])
            agg_acc[at, :] = part if first else agg_acc[at, :] + part
            return carry

        lax.fori_loop(0, rows // 256, step, 0)

    gather(2, True)
    from_sib.wait_recv()
    gather(3 - 2 * k)

    @pl.when(has_dn)
    def _():
        from_dn.wait_recv()

    @pl.when(has_up)
    def _():
        from_up.wait_recv()

    @pl.when(fwd_out)
    def _():
        f_fwd.start()

    gather(0)
    gather(4)

    @pl.when(fwd_in)
    def _():
        from_fwd.wait_recv()

    gather(1 + 2 * k)
    agg[...] = agg_acc[...].astype(BF16)
    agg_out = [
        remote(halves(agg, lax.rem(zp, 2)), agg_full.at[z], a_send.at[1, i], a_recv.at[1, i], (r, zp))
        for i, zp in enumerate(peers)
    ]
    for copy in agg_out:
        copy.start()
    agg_full[z] = agg[pl.ds(pl.multiple_of(lax.rem(z, 2) * half, half), half), :]

    def arrivals(buf, kind):
        return [
            remote(buf.at[zf], buf.at[zf], a_send.at[kind, i], a_recv.at[kind, i], (r, zf))
            for i, zf in enumerate(froms)
        ]

    for copy in arrivals(cot_full, 0) + arrivals(agg_full, 1):
        copy.wait_recv()

    tile = 256

    def hidden_part(w_a, w_b, base):
        def step(i, carry):
            hc = pl.ds(pl.multiple_of(i * tile, tile), tile)
            to = pl.ds(pl.multiple_of(base + i * tile, tile), tile)
            wa, wb = w_a[:, hc], w_b[:, hc]
            for m in range(half // tile):
                rs = slice(m * tile, (m + 1) * tile)
                x = jnp.concatenate([agg_full[q, rs] for q in range(n_rep)], axis=1)
                c = jnp.concatenate([cot_full[q, rs] for q in range(n_rep)], axis=1)
                value, slope = gelu_pair(dot(x, wa))
                hid[rs, to] = value.astype(BF16)
                gp[rs, to] = (dot(c, wb) * slope).astype(BF16)
            return carry

        lax.fori_loop(0, hidw // tile, step, 0)

    hidden_part(w_in_ref, w_out_ref, 0)
    for copy, fwd in zip(w_out1, w_fwd):
        copy.wait_recv()
        fwd.start()
    for copy in w_got:
        copy.wait_recv()
    hidden_part(w2_in, w2_out, hidw)

    def product(src, w_a, w_b, dst, zq):
        at = pl.ds(pl.multiple_of(zq * quarter, quarter), quarter)
        wa, wb = w_a[at, :], w_b[at, :]
        for m in range(half // tile):
            rs = slice(m * tile, (m + 1) * tile)
            res = dot(src[rs, :hidw], wa, ((1,), (1,))) + dot(src[rs, hidw:], wb, ((1,), (1,)))
            dst[zq, rs] = res.astype(BF16)

    def spread(src, w_a, w_b, part, landing, kind):
        sent = []
        for i, zp in enumerate(peers):
            product(src, w_a, w_b, part, zp)
            copy = remote(
                part.at[zp], landing.at[z], a_send.at[kind, i], a_recv.at[kind, i], (r, zp)
            )
            copy.start()
            sent.append(copy)
        product(src, w_a, w_b, part, z)
        landing[z] = part[z]
        return sent

    adj_out = spread(gp, w_in_ref, w2_in, adj_p, adj_in, 2)
    out_out = spread(hid, w_out_ref, w2_out, out_p, out_in, 3)

    for copy in arrivals(adj_in, 2):
        copy.wait_recv()
    for s in range(2):
        total = adj_in[s].astype(F32)
        for q in range(s + 2, n_rep, 2):
            total = total + adj_in[q].astype(F32)
        adj[s * half : (s + 1) * half] = total.astype(BF16)

    def piece(p, m):
        at = pl.ds(pl.multiple_of(p * rows + m * tile, tile), tile)
        return dot(dense_t[at, :], adj[...])

    def put(p, slot):
        def step(m, carry):
            at = pl.ds(pl.multiple_of(m * tile, tile), tile)
            c_send[slot, at, :] = piece(p, m).astype(BF16)
            return carry

        lax.fori_loop(0, rows // tile, step, 0)

    plain_to, helped_to = r - 2 + 4 * k, r + 2 - 4 * k
    c_help = remote(c_send.at[0], c_sib.at[0], c_sends.at[0], c_recvs.at[0], (sib, z))
    c_own = remote(c_send.at[1], c_sib.at[1], c_sends.at[1], c_recvs.at[1], (sib, z))
    c_plain = remote(
        c_send.at[2], c_nbr.at[1 - k], c_sends.at[2], c_recvs.at[3 - k], (plain_to, z)
    )
    c_helped = remote(
        c_send.at[3], c_nbr.at[k], c_sends.at[3], c_recvs.at[2 + k], (helped_to, z)
    )
    put(1 + 2 * k, 0)
    c_help.start()
    put(4 * k, 2)
    plain_ok, helped_ok = fwd_in, fwd_out

    @pl.when(plain_ok)
    def _():
        c_plain.start()

    c_help.wait_recv()

    def add_help(m, carry):
        at = pl.ds(pl.multiple_of(m * tile, tile), tile)
        total = piece(4 - 4 * k, m) + c_sib[0, at, :].astype(F32)
        c_send[3, at, :] = total.astype(BF16)
        return carry

    lax.fori_loop(0, rows // tile, add_help, 0)

    @pl.when(helped_ok)
    def _():
        c_helped.start()

    put(3 - 2 * k, 1)
    c_own.start()

    for copy in arrivals(out_in, 3):
        copy.wait_recv()
    for s in range(2):
        total = out_in[s].astype(F32)
        for q in range(s + 2, n_rep, 2):
            total = total + out_in[q].astype(F32)
        mine = ext[2 * rows + s * half : 2 * rows + (s + 1) * half]
        upd_ref[s * half : (s + 1) * half] = (mine.astype(F32) + total).astype(BF16)

    c_own.wait_recv()
    from_low = remote(c_nbr.at[0], c_nbr.at[0], c_sends.at[2], c_recvs.at[2], (r - 2, z))
    from_high = remote(c_nbr.at[1], c_nbr.at[1], c_sends.at[3], c_recvs.at[3], (r + 2, z))

    @pl.when(has_dn)
    def _():
        from_low.wait_recv()

    @pl.when(jnp.logical_not(has_dn))
    def _():
        c_nbr[0] = jnp.zeros((rows, quarter), BF16)

    @pl.when(has_up)
    def _():
        from_high.wait_recv()

    @pl.when(jnp.logical_not(has_up))
    def _():
        c_nbr[1] = jnp.zeros((rows, quarter), BF16)

    def finish(m, carry):
        at = pl.ds(pl.multiple_of(m * tile, tile), tile)
        total = piece(2, m) + c_sib[1, at, :].astype(F32)
        total = total + c_nbr[0, at, :].astype(F32) + c_nbr[1, at, :].astype(F32)
        grad_ref[at, :] = (cot_ref[at, :].astype(F32) + total).astype(BF16)
        return carry

    lax.fori_loop(0, rows // tile, finish, 0)

    for copy in cot_out + w_out1 + w_fwd + agg_out + adj_out + out_out + [f_sib, c_help, c_own]:
        copy.wait_send()
    for ok, copy in (
        (has_up, f_up), (has_dn, f_dn), (fwd_out, f_fwd), (plain_ok, c_plain), (helped_ok, c_helped)
    ):
        pl.when(ok)(copy.wait_send)


def body(n_row, n_rep, node_feats, block_cols, block_vals, w_in, w_out, cotangent):
    rows, quarter = cotangent.shape
    feat = node_feats.shape[1]
    row_blocks, slots = block_cols.shape
    hidw = w_in.shape[1]
    half = rows // 2
    first = (lax.axis_index("row") - 2) * row_blocks
    position = jnp.where(block_cols >= 0, block_cols - first, -1).reshape(1, -1, 1)
    landing = jnp.arange(5 * row_blocks, dtype=jnp.int32).reshape(-1, 1, 1)
    mask = jnp.broadcast_to(
        (position == landing).astype(F32), (5 * row_blocks, row_blocks * slots, 128)
    )
    vmem = pl.BlockSpec(memory_space=pltpu.VMEM)
    dma = pltpu.SemaphoreType.DMA
    return pl.pallas_call(
        functools.partial(kernel, n_row, n_rep),
        out_shape=(jax.ShapeDtypeStruct((rows, quarter), BF16),) * 2,
        in_specs=[vmem, pl.BlockSpec(memory_space=pl.ANY), vmem, vmem, vmem, vmem],
        out_specs=(vmem, vmem),
        scratch_shapes=[
            pltpu.VMEM((5 * rows, quarter), BF16),
            pltpu.VMEM((row_blocks, slots, 128, 128), BF16),
            pltpu.VMEM((rows, 5 * rows), BF16),
            pltpu.VMEM((5 * rows, rows), BF16),
            pltpu.VMEM((rows, quarter), F32),
            pltpu.VMEM((feat, hidw), BF16),
            pltpu.VMEM((feat, hidw), BF16),
            pltpu.VMEM((n_rep, half, quarter), BF16),
            pltpu.VMEM((rows, quarter), BF16),
            pltpu.VMEM((n_rep, half, quarter), BF16),
            pltpu.VMEM((half, 2 * hidw), BF16),
            pltpu.VMEM((half, 2 * hidw), BF16),
            pltpu.VMEM((n_rep, half, quarter), BF16),
            pltpu.VMEM((n_rep, half, quarter), BF16),
            pltpu.VMEM((n_rep, half, quarter), BF16),
            pltpu.VMEM((n_rep, half, quarter), BF16),
            pltpu.VMEM((rows, quarter), BF16),
            pltpu.VMEM((4, rows, quarter), BF16),
            pltpu.VMEM((2, rows, quarter), BF16),
            pltpu.VMEM((2, rows, quarter), BF16),
            dma,
            dma((4,)),
            dma((4,)),
            dma((4,)),
            dma((4,)),
            dma((4, n_rep - 1)),
            dma((4, n_rep - 1)),
            dma((4,)),
            dma((4,)),
        ],
        compiler_params=pltpu.CompilerParams(
            collective_id=0, has_side_effects=True, vmem_limit_bytes=60 * 1024 * 1024
        ),
    )(mask, node_feats, block_vals, w_in, w_out, cotangent)


def solution(mesh):
    in_specs = (
        P("row", None),
        P("row", None),
        P("row", None, None, None),
        P(None, "rep"),
        P(None, "rep"),
        P("row", "rep"),
    )
    out_specs = (P("row", "rep"), P("row", "rep"))
    run = functools.partial(body, mesh.shape["row"], mesh.shape["rep"])
    return jax.shard_map(run, mesh=mesh, in_specs=in_specs, out_specs=out_specs, check_vma=False)
```

time: 291 us -> 170 us (0.58)
  the two profiles are of different devices: /device:TPU:28 before, /device:TPU:11 now
where the time goes in v1:
time: 170 us
  Pallas kernels  163 us (96%)
  local copies, waits for them, and re-layouts  4.99 us (3%)
    pallas_call x1, Pallas kernels, body(): pl.pallas_call(functools.partial(kernel, n_row, n_rep), out_shape=(jax.Sh...  163 us
    unnamed x2, local copies, waits for them, and re-layouts  3.74 us

profile of v1, /device:TPU:11, one launch (start us, length us, event | category | flops | bytes accessed | tf_op | source)
XLA Modules:
  0.0 169.5 jit_solution(5817687570776590967)
XLA Ops:
  0.6 0.7 subtract_select_fusion
  1.3 0.1 copy.9
  1.4 0.1 eq.20
  1.5 1.1 broadcast_in_dim.10.mask_ref
  2.6 163.2 %shard_map.77 = (bf16[1024,256]{1,0:T(8,128)(2,1)}, bf16[1024,256]{1,0:T(8,128)(2,1)}) custom-call(f32[40,32,128]{2,1,0:T(8,128)} %broadcast_in_dim.10.mask_ref, bf16[1024,1024]{1,0:T(8,128)(2,1)} %feats_ref.1, bf16[8,4,128,128]{3,2,1,0:T(8,128)(2,1)} %vals_ref.1, bf16[1024,1024]{1,0:T(8,128)(2,1)} %w_in_ref.1, bf16[1024,1024]{1,0:T(8,128)(2,1)} %w_out_ref.1, ...), custom_call_target="tpu_custom_call" | custom-call | tf_op jit(solution)/shard_map/pallas_call | solution.py:383
  165.8 1.9 %copy.12 = bf16[1024,256]{1,0:T(8,128)(2,1)} copy(bf16[1024,256]{1,0:T(8,128)(2,1)} %get-tuple-element.4) | data formatting | bytes 1048576
  167.6 1.9 %copy.13 = bf16[1024,256]{1,0:T(8,128)(2,1)} copy(bf16[1024,256]{1,0:T(8,128)(2,1)} %get-tuple-element.5) | data formatting | bytes 1048576
  (1 shorter events, 0.0 us)

commit v2 on v1

--- a/solution.py
+++ b/solution.py
@@ -37,6 +37,8 @@
     k = lax.rem(r, 2)
     sib = r + 1 - 2 * k
     mate = z + 1 - 2 * lax.rem(z, 2)
+    bit2, bit4 = lax.rem(lax.div(r, 2), 2), lax.rem(lax.div(r, 4), 2)
+    near, far = r + 2 - 4 * bit2, r + 4 - 8 * bit4
     rows, quarter = cot_ref.shape
     half = rows // 2
     row_blocks = rows // 128
@@ -63,6 +65,8 @@
         pl.semaphore_signal(barrier, inc=1, device_id=(r, zp), device_id_type=MESH)
     pl.semaphore_signal(barrier, inc=1, device_id=(sib, z), device_id_type=MESH)
 
+    pl.semaphore_signal(barrier, inc=1, device_id=(far, z), device_id_type=MESH)
+
     @pl.when(has_up)
     def _():
         pl.semaphore_signal(barrier, inc=1, device_id=(r + 2, z), device_id_type=MESH)
@@ -75,7 +79,7 @@
     own_copy = pltpu.make_async_copy(feats_ref.at[:, columns], panel(ext, 2), loc_sem)
     own_copy.start()
     own_copy.wait()
-    pl.semaphore_wait(barrier, n_rep + has_up.astype(jnp.int32) + has_dn.astype(jnp.int32))
+    pl.semaphore_wait(barrier, n_rep + 1 + has_up.astype(jnp.int32) + has_dn.astype(jnp.int32))
 
     own = panel(ext, 2)
     f_up = remote(own, panel(ext, 0), f_send.at[0], f_recv.at[0], (r + 2, z))
@@ -104,22 +108,44 @@
         remote(halves(cot_ref, lax.rem(zp, 2)), cot_full.at[z], a_send.at[0, i], a_recv.at[0, i], (r, zp))
         for i, zp in enumerate(peers)
     ]
-    for copy in cot_out:
-        copy.start()
-    w_out1 = [
-        remote(halves(src, k), halves(dst, k), w_send.at[i], w_recv.at[i], (r, mate))
-        for i, (src, dst) in enumerate(((w_in_ref, w2_in), (w_out_ref, w2_out)))
+    eighth = feat // 8
+    quad, pair = 4 * k, 4 * k + 2 * bit2
+
+    def span(ref, start, count):
+        return ref.at[pl.ds(pl.multiple_of(start * eighth, eighth), count * eighth)]
+
+    def round_of(step, start, count, dev, first=False):
+        ends = ((w_in_ref if first else w2_in, w2_in), (w_out_ref if first else w2_out, w2_out))
+        return [
+            remote(
+                span(src, start, count), span(dst, start, count),
+                w_send.at[2 * step + i], w_recv.at[2 * step + i], dev,
+            )
+            for i, (src, dst) in enumerate(ends)
+        ]
+
+    w_rounds = [
+        round_of(0, pair + bit4, 1, (r, mate), True),
+        round_of(1, pair + bit4, 1, (far, z)),
+        round_of(2, pair, 2, (near, z)),
+        round_of(3, quad, 4, (sib, z)),
     ]
-    w_fwd = [
-        remote(halves(dst, k), halves(dst, k), w_send.at[2 + i], w_recv.at[2 + i], (sib, z))
-        for i, dst in enumerate((w2_in, w2_out))
+    w_lands = [
+        w_rounds[0],
+        round_of(1, pair + 1 - bit4, 1, (far, z)),
+        round_of(2, quad + 2 - 2 * bit2, 2, (near, z)),
+        round_of(3, 4 - quad, 4, (sib, z)),
     ]
-    w_got = [
-        remote(halves(dst, 1 - k), halves(dst, 1 - k), w_send.at[2 + i], w_recv.at[2 + i], (sib, z))
-        for i, dst in enumerate((w2_in, w2_out))
-    ]
-    for copy in w_out1:
-        copy.start()
+
+    def pass_weights(step):
+        if step:
+            for copy in w_lands[step - 1]:
+                copy.wait_recv()
+        if step < 4:
+            for copy in w_rounds[step]:
+                copy.start()
+
+    pass_weights(0)
 
     @pl.when(jnp.logical_not(has_dn))
     def _():
@@ -161,6 +187,9 @@
         return carry
 
     lax.fori_loop(0, 5 * row_blocks, fill_dense, 0)
+    pass_weights(1)
+    for copy in cot_out:
+        copy.start()
 
     def gather(slot, first=False):
         inner = pl.ds(pl.multiple_of(slot * rows, rows), rows)
@@ -189,6 +218,7 @@
     def _():
         f_fwd.start()
 
+    pass_weights(2)
     gather(0)
     gather(4)
 
@@ -212,6 +242,7 @@
             for i, zf in enumerate(froms)
         ]
 
+    pass_weights(3)
     for copy in arrivals(cot_full, 0) + arrivals(agg_full, 1):
         copy.wait_recv()
 
@@ -234,11 +265,7 @@
         lax.fori_loop(0, hidw // tile, step, 0)
 
     hidden_part(w_in_ref, w_out_ref, 0)
-    for copy, fwd in zip(w_out1, w_fwd):
-        copy.wait_recv()
-        fwd.start()
-    for copy in w_got:
-        copy.wait_recv()
+    pass_weights(4)
     hidden_part(w2_in, w2_out, hidw)
 
     def product(src, w_a, w_b, dst, zq):
@@ -358,7 +385,7 @@
 
     lax.fori_loop(0, rows // tile, finish, 0)
 
-    for copy in cot_out + w_out1 + w_fwd + agg_out + adj_out + out_out + [f_sib, c_help, c_own]:
+    for copy in cot_out + sum(w_rounds, []) + agg_out + adj_out + out_out + [f_sib, c_help, c_own]:
         copy.wait_send()
     for ok, copy in (
         (has_up, f_up), (has_dn, f_dn), (fwd_out, f_fwd), (plain_ok, c_plain), (helped_ok, c_helped)
@@ -409,8 +436,8 @@
             dma,
             dma((4,)),
             dma((4,)),
-            dma((4,)),
-            dma((4,)),
+            dma((8,)),
+            dma((8,)),
             dma((4, n_rep - 1)),
             dma((4, n_rep - 1)),
             dma((4,)),

time: 170 us -> 147 us (0.86)
  the two profiles are of different devices: /device:TPU:11 before, /device:TPU:28 now
where the time goes in v2:
time: 147 us; the launch traced here: 146 us
  Pallas kernels  140 us (95%)
  local copies, waits for them, and re-layouts  4.99 us (3%)
    pallas_call x1, Pallas kernels, body(): pl.pallas_call(functools.partial(kernel, n_row, n_rep), out_shape=(jax.Sh...  140 us
    unnamed x2, local copies, waits for them, and re-layouts  3.74 us

profile of v2, /device:TPU:28, one launch (start us, length us, event | category | flops | bytes accessed | tf_op | source)
XLA Modules:
  0.0 146.3 jit_solution(9515999087649081946)
XLA Ops:
  0.6 0.7 subtract_select_fusion
  1.3 0.1 copy.9
  1.4 0.1 eq.20
  1.5 1.1 broadcast_in_dim.10.mask_ref
  2.6 140.0 %shard_map.77 = (bf16[1024,256]{1,0:T(8,128)(2,1)}, bf16[1024,256]{1,0:T(8,128)(2,1)}) custom-call(f32[40,32,128]{2,1,0:T(8,128)} %broadcast_in_dim.10.mask_ref, bf16[1024,1024]{1,0:T(8,128)(2,1)} %feats_ref.1, bf16[8,4,128,128]{3,2,1,0:T(8,128)(2,1)} %vals_ref.1, bf16[1024,1024]{1,0:T(8,128)(2,1)} %w_in_ref.1, bf16[1024,1024]{1,0:T(8,128)(2,1)} %w_out_ref.1, ...), custom_call_target="tpu_custom_call" | custom-call | tf_op jit(solution)/shard_map/pallas_call | solution.py:410
  142.6 1.9 %copy.12 = bf16[1024,256]{1,0:T(8,128)(2,1)} copy(bf16[1024,256]{1,0:T(8,128)(2,1)} %get-tuple-element.4) | data formatting | bytes 1048576
  144.4 1.9 %copy.13 = bf16[1024,256]{1,0:T(8,128)(2,1)} copy(bf16[1024,256]{1,0:T(8,128)(2,1)} %get-tuple-element.5) | data formatting | bytes 1048576
  (1 shorter events, 0.0 us)

commit v3 on v2

--- a/solution.py
+++ b/solution.py
@@ -276,24 +276,26 @@
             res = dot(src[rs, :hidw], wa, ((1,), (1,))) + dot(src[rs, hidw:], wb, ((1,), (1,)))
             dst[zq, rs] = res.astype(BF16)
 
-    def spread(src, w_a, w_b, part, landing, kind):
-        sent = []
-        for i, zp in enumerate(peers):
-            product(src, w_a, w_b, part, zp)
-            copy = remote(
-                part.at[zp], landing.at[z], a_send.at[kind, i], a_recv.at[kind, i], (r, zp)
-            )
-            copy.start()
-            sent.append(copy)
-        product(src, w_a, w_b, part, z)
-        landing[z] = part[z]
-        return sent
-
-    adj_out = spread(gp, w_in_ref, w2_in, adj_p, adj_in, 2)
-    out_out = spread(hid, w_out_ref, w2_out, out_p, out_in, 3)
+    def to_peer(part, landing, kind, i):
+        return remote(
+            part.at[peers[i]], landing.at[z], a_send.at[kind, i], a_recv.at[kind, i], (r, peers[i])
+        )
+
+    adj_out = [to_peer(adj_p, adj_in, 2, i) for i in range(n_rep - 1)]
+    out_out = [to_peer(out_p, out_in, 3, i) for i in range(n_rep - 1)]
+    for i, zp in enumerate(peers):
+        product(gp, w_in_ref, w2_in, adj_p, zp)
+        adj_out[i].start()
+    product(gp, w_in_ref, w2_in, adj_p, z)
+    adj_in[z] = adj_p[z]
+    for zp in peers + [z]:
+        product(hid, w_out_ref, w2_out, out_p, zp)
+    out_in[z] = out_p[z]
 
     for copy in arrivals(adj_in, 2):
         copy.wait_recv()
+    for copy in out_out:
+        copy.start()
     for s in range(2):
         total = adj_in[s].astype(F32)
         for q in range(s + 2, n_rep, 2):

time: 147 us -> 147 us (level)
  no operation moved by 1% of the time
where the time goes in v3:
time: 147 us; the launch traced here: 146 us
  Pallas kernels  140 us (95%)
  local copies, waits for them, and re-layouts  4.99 us (3%)
    pallas_call x1, Pallas kernels, body(): pl.pallas_call(functools.partial(kernel, n_row, n_rep), out_shape=(jax.Sh...  140 us
    unnamed x2, local copies, waits for them, and re-layouts  3.74 us

profile of v3, /device:TPU:28, one launch (start us, length us, event | category | flops | bytes accessed | tf_op | source)
XLA Modules:
  0.0 146.3 jit_solution(6733677943209435231)
XLA Ops:
  0.6 0.7 subtract_select_fusion
  1.3 0.1 copy.9
  1.4 0.1 eq.20
  1.5 1.1 broadcast_in_dim.10.mask_ref
  2.6 140.0 %shard_map.77 = (bf16[1024,256]{1,0:T(8,128)(2,1)}, bf16[1024,256]{1,0:T(8,128)(2,1)}) custom-call(f32[40,32,128]{2,1,0:T(8,128)} %broadcast_in_dim.10.mask_ref, bf16[1024,1024]{1,0:T(8,128)(2,1)} %feats_ref.1, bf16[8,4,128,128]{3,2,1,0:T(8,128)(2,1)} %vals_ref.1, bf16[1024,1024]{1,0:T(8,128)(2,1)} %w_in_ref.1, bf16[1024,1024]{1,0:T(8,128)(2,1)} %w_out_ref.1, ...), custom_call_target="tpu_custom_call" | custom-call | tf_op jit(solution)/shard_map/pallas_call | solution.py:412
  142.6 1.9 %copy.12 = bf16[1024,256]{1,0:T(8,128)(2,1)} copy(bf16[1024,256]{1,0:T(8,128)(2,1)} %get-tuple-element.4) | data formatting | bytes 1048576
  144.5 1.9 %copy.13 = bf16[1024,256]{1,0:T(8,128)(2,1)} copy(bf16[1024,256]{1,0:T(8,128)(2,1)} %get-tuple-element.5) | data formatting | bytes 1048576
  (1 shorter events, 0.0 us)
